TPU v7x, 256 devices: a whole 4x4x8 slice. The times are simulated.
256 devices in a mesh: grp: 8 (over z), tile: 32 (over x, y, core).
Axes of the slice: x: 4, y: 4, z: 8, core: 2. Of those that a mesh axis runs over, the one named last changes fastest.
Arguments:
- speed: float32 [128, 2, 32, 128], P('tile'), may hold values from 0.15 to 0.4
- density: float32 [128, 2, 32, 128], P('tile'), may hold values from 1 to 3
- fwd_state: bfloat16 [256, 4, 32, 32, 128], P(('grp', 'tile')), may hold values from -6 to 6
- adj_state: bfloat16 [256, 4, 32, 32, 128], P(('grp', 'tile')), may hold values from -6 to 6
- aperture: int32 [256, 16], P(('grp', 'tile')), may hold values from 0 to 127, as said below
- src_pos: int32 [256, 3], P(('grp', 'tile')), may hold values from 0 to 127, as said below
- wavelet: float32 [256, 4], P(('grp', 'tile')), may hold values from -15 to 15
- rec_pos: int32 [256, 32, 2], P(('grp', 'tile')), may hold values from 0 to 127, as said below
- residual: float32 [256, 4, 32], P(('grp', 'tile')), may hold values from -6 to 6
Outputs:
- grad_speed: float32 [128, 2, 32, 128], P('tile')
- grad_density: float32 [128, 2, 32, 128], P('tile')
Inputs may be any that keep to these rules, and one draw needn't show every extreme that they name: `aperture`: row s is (c + j) * 4 + e for j = 0 .. 15, with one c in 0 .. 16 and one e in 0 .. 3 for each shot, so a shot takes exactly one tile from each of 16 owners. `src_pos`: columns are x in 0 .. 31, y in 0 .. 31, z in 0 .. 127. `rec_pos`: columns are y in 0 .. 31 and z in 0 .. 127.
All inputs are finite; a program needn't handle non-finite values.
Results may differ from a plain program's by a relative error of at most 0.0003.
Values sent between devices are 32-bit elements; how exact they have to be, the bound alone decides.
A program may use at most 64 MiB of HBM per device.

v0:
```python
import math
import jax
import jax.numpy as jnp
from jax import lax
from jax.sharding import PartitionSpec as P

COEF = (1225.0 / 1024.0, -245.0 / 3072.0, 49.0 / 5120.0, -5.0 / 7168.0)


def padded_along(values, which_dim):
    widths = [(0, 0), (0, 0), (0, 0)]
    widths[which_dim] = (4, 4)
    return jnp.pad(values, widths)


def forward_diff(values, which_dim):
    length = values.shape[which_dim]
    padded = padded_along(values, which_dim)
    total = jnp.zeros_like(values)
    for order in range(1, 5):
        upper = lax.slice_in_dim(padded, 4 + order, 4 + order + length, axis=which_dim)
        lower = lax.slice_in_dim(padded, 5 - order, 5 - order + length, axis=which_dim)
        total = total + COEF[order - 1] * (upper - lower)
    return total


def backward_diff(values, which_dim):
    length = values.shape[which_dim]
    padded = padded_along(values, which_dim)
    total = jnp.zeros_like(values)
    for order in range(1, 5):
        upper = lax.slice_in_dim(padded, 3 + order, 3 + order + length, axis=which_dim)
        lower = lax.slice_in_dim(padded, 4 - order, 4 - order + length, axis=which_dim)
        total = total + COEF[order - 1] * (upper - lower)
    return total


def advance(pressure, velocity, bulk, buoyancy, source):
    moved = tuple(
        (
            velocity[which_dim] + buoyancy * forward_diff(pressure, which_dim)
            for which_dim in range(3)
        )
    )
    divergence = (
        backward_diff(moved[0], 0) + backward_diff(moved[1], 1) + backward_diff(moved[2], 2)
    )
    return (pressure + bulk * divergence + source, moved)


def evolve(speed_ap, density_ap, fwd_state, adj_state, src_pos, wavelet, rec_pos, residual):
    bulk = density_ap * speed_ap * speed_ap
    buoyancy = 1.0 / density_ap
    xs_cells = jnp.arange(speed_ap.shape[0], dtype=jnp.int32)
    ys_cells = jnp.arange(speed_ap.shape[1], dtype=jnp.int32)
    zs_cells = jnp.arange(speed_ap.shape[2], dtype=jnp.int32)
    src_mask = (
        (xs_cells == src_pos[0])[:, None, None]
        & (ys_cells == src_pos[1])[None, :, None]
        & (zs_cells == src_pos[2])[None, None, :]
    ).astype(jnp.float32)
    rec_mask = (
        (ys_cells[None, :, None] == rec_pos[:, 0][:, None, None])
        & (zs_cells[None, None, :] == rec_pos[:, 1][:, None, None])
    ).astype(jnp.float32)
    state = fwd_state.astype(jnp.float32)
    pressure = state[0]
    velocity = (state[1], state[2], state[3])
    changes = []
    steps_count = wavelet.shape[0]
    for step_index in range(steps_count):
        new_pressure, new_velocity = advance(
            pressure, velocity, bulk, buoyancy, wavelet[step_index] * src_mask
        )
        changes.append(
            (new_pressure - pressure, tuple((new_velocity[d] - velocity[d] for d in range(3))))
        )
        pressure, velocity = (new_pressure, new_velocity)
    adjoint = adj_state.astype(jnp.float32)
    adj_pressure = adjoint[0]
    adj_velocity = (adjoint[1], adjoint[2], adjoint[3])
    bulk_image = jnp.zeros_like(bulk)
    buoy_image = jnp.zeros_like(bulk)
    for step_index in reversed(range(steps_count)):
        adj_pressure, adj_velocity = advance(
            adj_pressure,
            adj_velocity,
            bulk,
            buoyancy,
            residual[step_index][:, None, None] * rec_mask,
        )
        bulk_image = bulk_image + changes[step_index][0] * adj_pressure
        dvel = changes[step_index][1]
        buoy_image = (
            buoy_image
            + dvel[0] * adj_velocity[0]
            + dvel[1] * adj_velocity[1]
            + dvel[2] * adj_velocity[2]
        )
    return (bulk_image, buoy_image)


def per_device(speed, density, fwd_state, adj_state, aperture, src_pos, wavelet, rec_pos, residual):
    owners = lax.axis_size("tile")
    myself = lax.axis_index("tile")
    held = speed.shape[0]
    tile_x, tile_y, depth = (speed.shape[1], speed.shape[2], speed.shape[3])
    stripes = aperture.shape[1]
    mine = aperture[0]
    lists = lax.all_gather(aperture, "tile", axis=0, tiled=True)
    owner_ids = jnp.arange(owners, dtype=jnp.int32)
    held_ids = jnp.arange(held, dtype=jnp.int32)
    matches = (lists // held == myself)[:, :, None] & (
        (lists % held)[:, :, None] == held_ids[None, None, :]
    )
    picked = jnp.sum(matches.astype(jnp.float32), axis=1)
    placed = (mine[:, None] // held == owner_ids[None, :]).astype(jnp.float32)
    highest = lax.Precision.HIGHEST
    pieces = (
        lax.all_gather(speed, "tile", axis=0, tiled=True),
        lax.all_gather(density, "tile", axis=0, tiled=True),
    )
    rows = pieces[0].shape[0]
    select = (mine[:, None] == jnp.arange(rows, dtype=jnp.int32)[None, :]).astype(jnp.float32)
    ap_speed = jnp.einsum("jt,txyz->jxyz", select, pieces[0], precision=highest)
    ap_density = jnp.einsum("jt,txyz->jxyz", select, pieces[1], precision=highest)
    speed_ap = ap_speed.reshape(stripes * tile_x, tile_y, depth)
    density_ap = ap_density.reshape(stripes * tile_x, tile_y, depth)
    bulk_image, buoy_image = evolve(
        speed_ap,
        density_ap,
        fwd_state[0],
        adj_state[0],
        src_pos[0],
        wavelet[0],
        rec_pos[0],
        residual[0],
    )
    bulk_parts = bulk_image.reshape(stripes, tile_x, tile_y, depth)
    buoy_parts = buoy_image.reshape(stripes, tile_x, tile_y, depth)
    back_bulk = jnp.einsum("jo,jxyz->oxyz", placed, bulk_parts, precision=highest)
    back_buoy = jnp.einsum("jo,jxyz->oxyz", placed, buoy_parts, precision=highest)
    came_bulk, came_buoy = (
        lax.all_to_all(back_bulk, "tile", split_axis=0, concat_axis=0, tiled=True),
        lax.all_to_all(back_buoy, "tile", split_axis=0, concat_axis=0, tiled=True),
    )
    own_bulk = jnp.einsum("rt,rxyz->txyz", picked, came_bulk, precision=highest)
    own_buoy = jnp.einsum("rt,rxyz->txyz", picked, came_buoy, precision=highest)
    bulk_sum, buoy_sum = lax.psum((own_bulk, own_buoy), "grp")
    scale = 1.0 / math.sqrt(lax.axis_size("grp") * owners)
    grad_speed = scale * (bulk_sum * (2.0 * density * speed))
    grad_density = scale * (bulk_sum * (speed * speed) - buoy_sum / (density * density))
    return (grad_speed, grad_density)


def solution(mesh):
    return jax.shard_map(
        per_device,
        mesh=mesh,
        in_specs=(
            P("tile", None, None, None),
            P("tile", None, None, None),
            P(("grp", "tile"), None, None, None, None),
            P(("grp", "tile"), None, None, None, None),
            P(("grp", "tile"), None),
            P(("grp", "tile"), None),
            P(("grp", "tile"), None),
            P(("grp", "tile"), None, None),
            P(("grp", "tile"), None, None),
        ),
        out_specs=(P("tile", None, None, None), P("tile", None, None, None)),
        check_vma=False,
    )
```

profile of v0, /device:TPU:2, one launch (start us, length us, event | category | flops | bytes accessed | tf_op | source)
XLA Modules:
  0.0 306.5 jit_solution(4750725316067010165)
XLA Ops:
  7.2 0.0 copy-start.8
  7.2 0.0 copy-start.6
  7.2 0.0 copy-start.7
  7.2 0.0 copy-start.10
  7.2 0.0 copy-start.9
  7.2 0.0 all-gather.4.cloned.1.call-start
  7.3 0.7 all-gather.4.cloned.1.call-update
  8.0 0.0 all-gather.6.cloned.1.call-start
  8.0 0.7 all-gather.6.cloned.1.call-update
  8.7 1.5 convert_element_type.67
  10.2 1.5 convert_element_type.68
  11.7 0.0 copy-done.8
  11.7 0.0 copy-start
  11.7 0.7 fusion.658
  12.5 0.6 iota_compare_fusion.5
  13.1 1.3 iota_compare_fusion.6
  14.4 0.0 copy-done.6
  14.4 0.7 fusion.657
  15.1 0.0 copy-done.7
  15.1 0.0 copy-done.10
  15.1 0.1 iota_compare_fusion.1
  15.2 0.1 iota_compare_fusion.2
  15.3 0.1 broadcast_and_fusion
  15.4 0.0 copy-done
  15.4 0.9 slice_bitcast_fusion.3
  16.2 48.1 %all-gather.4.cloned.1.call-done = f32[128,2,32,128]{3,2,1,0:T(8,128)} async-done(((f32[4,2,32,128]{3,2,1,0:T(8,128)}), f32[128,2,32,128]{3,2,1,0:T(8,128)}) %all-gather.4.cloned.1.call-update) | async-done | bytes 4194320 | tf_op jit(solution)/shard_map/all_gather | solution.py:121
  64.4 5.8 %fusion.2 = f32[16,2,32,128]{3,0,2,1:T(8,128)S(1)} fusion(f32[128,2,32,128]{3,2,1,0:T(8,128)} %all-gather.4.cloned.1.call-done, s32[16]{0:T(128)S(1)} %bitcast.173), kind=kOutput, calls=%fused_computation.2 | convolution fusion | flops 201328640 | bytes 4718656 | tf_op jit(solution)/shard_map/jt,txyz->jxyz/dot_general | solution.py:126
  70.2 0.2 copy.73
  70.4 47.1 %all-gather.6.cloned.1.call-done = f32[128,2,32,128]{3,2,1,0:T(8,128)} async-done(((f32[4,2,32,128]{3,2,1,0:T(8,128)}), f32[128,2,32,128]{3,2,1,0:T(8,128)}) %all-gather.6.cloned.1.call-update) | async-done | bytes 4194320 | tf_op jit(solution)/shard_map/all_gather | solution.py:120
  117.5 6.0 %fusion = f32[16,2,32,128]{3,0,2,1:T(8,128)S(1)} fusion(f32[128,2,32,128]{3,2,1,0:T(8,128)} %all-gather.6.cloned.1.call-done, s32[16]{0:T(128)S(1)} %bitcast.174), kind=kOutput, calls=%fused_computation | convolution fusion | flops 201328640 | bytes 4718656 | tf_op jit(solution)/shard_map/jt,txyz->jxyz/dot_general | solution.py:125
  123.5 0.2 copy.75
  123.7 3.0 fusion.540
  126.7 2.3 fusion.30
  129.0 1.6 fusion.247
  130.6 2.8 fusion.313
  133.4 1.6 fusion.300
  135.0 2.2 fusion.83
  137.2 2.8 fusion.337
  140.0 1.6 fusion.353
  141.6 2.2 fusion.136
  143.8 4.9 %multiply_add_fusion = (f32[32,32,128]{2,1,0:T(8,128)}, f32[32,32,128]{2,1,0:T(8,128)}, f32[32,32,128]{2,1,0:T(8,128)}, f32[32,32,128]{2,1,0:T(8,128)}, f32[32,3...) fusion(f32[32,32,128]{2,1,0:T(8,128)S(1)} %get-tuple-element.49, ...), kind=kLoop, calls=%fused_computation.988 | loop fusion | flops 14942208 | bytes 16252928 | tf_op jit(solution)/shard_map/add | solution.py:95
  148.7 14.3 %fusion.194 = f32[32,32,128]{2,1,0:T(8,128)S(1)} fusion(f32[32,32,128]{2,1,0:T(8,128)S(1)} %fusion.247, f32[32,32,128]{2,1,0:T(8,128)S(1)} %fusion.136, f32[32,32,128]{2,1,0:T(8,128)S(1)} %get-tuple-element.22, f32[32,32,128]{2,1,0:T(8,128)} %get-tuple-element.20, f32[32,32,128]{2,1,0:T(8,128)} %get-tuple-element.19, f32[32,32,128]{2,1,0:T(8,128)S(1)} %fusion.353, ...), kind=kLoop, calls=%fused_computation.539 | loop fusion | flops 11927552 | bytes 7870724 | tf_op jit(solution)/shard_map/add | solution.py:92
  163.1 0.9 fusion.632
  164.0 1.6 copy.77
  165.6 5.9 %all-to-all-start = ((f32[32,2,32,128]{3,2,1,0:T(8,128)}), f32[32,2,32,128]{3,2,1,0:T(8,128)S(1)}, u32[]{:S(2)}, u32[]{:S(2)}) async-start(f32[32,2,32,128]{3,2,1,0:T(8,128)} %copy.77), calls=%async_computation | async-start | bytes 2097152 | tf_op jit(solution)/shard_map/all_to_all | solution.py:144
  171.4 0.0 copy-done.2
  171.4 0.0 copy-start.4
  171.5 0.0 copy-start.5
  171.5 0.9 fusion.630
  172.4 1.6 copy.84
  173.9 11.9 %all-to-all-done = f32[32,2,32,128]{3,2,1,0:T(8,128)S(1)} async-done(((f32[32,2,32,128]{3,2,1,0:T(8,128)}), f32[32,2,32,128]{3,2,1,0:T(8,128)S(1)}, u32[]{:S(2)}, u32[]{:S(2)}) %all-to-all-start) | async-done | bytes 1048608 | tf_op jit(solution)/shard_map/all_to_all | solution.py:144
  185.9 6.4 %all-to-all-start.1 = ((f32[32,2,32,128]{3,2,1,0:T(8,128)}), f32[32,2,32,128]{3,2,1,0:T(8,128)S(1)}, u32[]{:S(2)}, u32[]{:S(2)}) async-start(f32[32,2,32,128]{3,2,1,0:T(8,128)} %copy.84), calls=%async_computation.1 | async-start | bytes 2097152 | tf_op jit(solution)/shard_map/all_to_all | solution.py:145
  192.3 0.0 all-reduce.51.cloned.1.call-start
  192.4 29.0 %all-gather = s32[32,1,16]{2,1,0:T(1,128)S(1)} all-gather(s32[1,1,16]{2,1,0:T(1,128)S(1)} %bitcast.175), channel_id=1, replica_groups=mesh['grp'=8,'tile'=32] {'tile'}, dimensions={0}, use_global_device_ids=true | all-gather | bytes 2112 | tf_op jit(solution)/shard_map/all_gather | solution.py:110
  221.4 0.1 copy.71
  221.5 1.8 fusion.6
  223.3 0.0 all-to-all-done.1
  223.3 1.8 fusion.4
  225.1 0.0 all-reduce.51.cloned.1.call-update
  225.2 72.3 %all-reduce.51.cloned.1.call-done = (f32[4,2,32,128]{3,0,2,1:T(4,128)}, f32[4,2,32,128]{3,0,2,1:T(4,128)}) async-done(((f32[4,2,32,128]{3,0,2,1:T(4,128)}, f32[4,2,32,128]{3,0,2,1:T(4,128)}), (f32[4,2,32,128]{3,0,2,1:T(4,128)}, f32[4,2,32,128]{3,0,2,1:T(4,128)})) %all-reduce.51.cloned.1.call-update) | async-done | bytes 262160 | tf_op jit(solution)/shard_map/psum | solution.py:149
  297.5 0.0 copy-done.5
  297.5 1.2 subtract_multiply_fusion
  298.7 0.7 copy.88
  299.3 0.7 copy.89
  (13 shorter events, 0.1 us)
Async XLA Ops:
  7.2 4.6 %copy-start.8 = (s32[1,3]{1,0:T(1,128)S(1)}, s32[1,3]{1,0:T(1,128)}, u32[]{:S(2)}) copy-start(s32[1,3]{1,0:T(1,128)} %param.14) | copy-start | bytes 40
  7.2 7.2 %copy-start.6 = (f32[1,4]{1,0:T(1,128)S(1)}, f32[1,4]{1,0:T(1,128)}, u32[]{:S(2)}) copy-start(f32[1,4]{1,0:T(1,128)} %param.15) | copy-start | bytes 52
  7.2 7.9 %copy-start.7 = (s32[1,16]{1,0:T(1,128)S(1)}, s32[1,16]{1,0:T(1,128)}, u32[]{:S(2)}) copy-start(s32[1,16]{1,0:T(1,128)} %param.13) | copy-start | bytes 196
  7.2 7.9 %copy-start.10 = (s32[1,32,2]{1,2,0:T(2,128)S(1)}, s32[1,32,2]{1,2,0:T(2,128)}, u32[]{:S(2)}) copy-start(s32[1,32,2]{1,2,0:T(2,128)} %param.16) | copy-start | bytes 772
  7.2 7.9 %copy-start.9 = (f32[1,4,32]{2,1,0:T(4,128)S(1)}, f32[1,4,32]{2,1,0:T(4,128)}, u32[]{:S(2)}) copy-start(f32[1,4,32]{2,1,0:T(4,128)} %param.17) | copy-start | bytes 1540
  7.2 57.1 %all-gather.4.cloned.1.call-start = ((), (), s32[]{:S(2)}) async-start(), calls=%async_computation.2 | async-start | bytes 4325376 | tf_op jit(solution)/shard_map/all_gather | solution.py:121
  8.0 109.5 %all-gather.6.cloned.1.call-start = ((), (), s32[]{:S(2)}) async-start(), calls=%async_computation.3 | async-start | bytes 4325376 | tf_op jit(solution)/shard_map/all_gather | solution.py:120
  11.7 3.6 %copy-start = (f32[1,4,32,32,128]{4,3,2,1,0:T(8,128)}, f32[1,4,32,32,128]{4,3,2,1,0:T(8,128)S(1)}, u32[]{:S(2)}) copy-start(f32[1,4,32,32,128]{4,3,2,1,0:T(8,128)S(1)} %convert_element_type.68) | copy-start | bytes 6291460
  117.5 6.2 %copy-start.1 = (f32[1,4,32,32,128]{4,3,2,1,0:T(8,128)S(1)}, f32[1,4,32,32,128]{4,3,2,1,0:T(8,128)}, u32[]{:S(2)}) copy-start(f32[1,4,32,32,128]{4,3,2,1,0:T(8,128)} %copy-done) | copy-start | bytes 6291460
  117.5 6.2 %copy-start.3 = (f32[32,32,128]{2,1,0:T(8,128)S(1)}, f32[32,32,128]{2,1,0:T(8,128)}, u32[]{:S(2)}) copy-start(f32[32,32,128]{2,1,0:T(8,128)} %get-tuple-element.66) | copy-start | bytes 1572868
  163.1 8.4 %copy-start.2 = (f32[32,32,128]{2,1,0:T(8,128)S(1)}, f32[32,32,128]{2,1,0:T(8,128)}, u32[]{:S(2)}) copy-start(f32[32,32,128]{2,1,0:T(8,128)} %get-tuple-element.14) | copy-start | bytes 1572868
  165.6 20.3 %all-to-all-start = ((f32[32,2,32,128]{3,2,1,0:T(8,128)}), f32[32,2,32,128]{3,2,1,0:T(8,128)S(1)}, u32[]{:S(2)}, u32[]{:S(2)}) async-start(f32[32,2,32,128]{3,2,1,0:T(8,128)} %copy.77), calls=%async_computation | async-start | bytes 2097152 | tf_op jit(solution)/shard_map/all_to_all | solution.py:144
  171.4 126.0 %copy-start.4 = (f32[4,2,32,128]{3,2,1,0:T(8,128)S(1)}, f32[4,2,32,128]{3,2,1,0:T(8,128)}, u32[]{:S(2)}) copy-start(f32[4,2,32,128]{3,2,1,0:T(8,128)} %param.10) | copy-start | bytes 393220
  171.5 126.0 %copy-start.5 = (f32[4,2,32,128]{3,2,1,0:T(8,128)S(1)}, f32[4,2,32,128]{3,2,1,0:T(8,128)}, u32[]{:S(2)}) copy-start(f32[4,2,32,128]{3,2,1,0:T(8,128)} %param.9) | copy-start | bytes 393220
  185.9 37.5 %all-to-all-start.1 = ((f32[32,2,32,128]{3,2,1,0:T(8,128)}), f32[32,2,32,128]{3,2,1,0:T(8,128)S(1)}, u32[]{:S(2)}, u32[]{:S(2)}) async-start(f32[32,2,32,128]{3,2,1,0:T(8,128)} %copy.84), calls=%async_computation.1 | async-start | bytes 2097152 | tf_op jit(solution)/shard_map/all_to_all | solution.py:145
  192.3 105.2 %all-reduce.51.cloned.1.call-start = ((), (), s32[]{:S(2)}) async-start(), calls=%async_computation.4 | async-start | bytes 524288 | tf_op jit(solution)/shard_map/psum | solution.py:149
Sparse Core Ops, SparseCore 0:
  10.6 53.7 all-gather.3
  66.9 50.5 all-gather.5
  225.3 72.1 all-reduce.50
where the time goes:
time: 307 us
  waiting for transfers between devices  181 us (59%)
  other arithmetic  45.7 us (15%)
  blocking collectives  29 us (9%)
  matrix products  17.3 us (6%)
  between operations  14.1 us (5%)
  starting transfers between devices  12.4 us (4%)
  local copies, waits for them, and re-layouts  7.24 us (2%)
    psum x1, waiting for transfers between devices, per_device(): bulk_sum, buoy_sum = lax.psum((own_bulk, own_buoy), 'grp')  72.3 us
    all_gather x1, waiting for transfers between devices, per_device(): lax.all_gather(density, 'tile', axis=0, tiled=True)  48.1 us
    all_gather x1, waiting for transfers between devices, per_device(): lax.all_gather(speed, 'tile', axis=0, tiled=True)  47.1 us
    all_gather x1, blocking collectives, per_device(): lists = lax.all_gather(aperture, 'tile', axis=0, tiled=True)  29 us
    add x1, other arithmetic, evolve(): bulk_image = bulk_image + changes[step_index][0] * adj_pressure  14.3 us
    all_to_all x1, waiting for transfers between devices, per_device(): lax.all_to_all(back_bulk, 'tile', split_axis=0, concat_axis=0, tiled=True)  11.9 us
    add x6, other arithmetic, advance(): return (pressure + bulk * divergence + source, moved)  11.4 us
    add x3, other arithmetic, advance(): velocity[which_dim] + buoyancy * forward_diff(pressure, which_dim)  8.67 us
  transfers between devices with their start and end apart: 5, of which 4 were waited for; matrix products, arithmetic and copies ran while one was open for 6% of the time, Pallas kernels for 0%

commit v1 on v0

--- a/solution.py
+++ b/solution.py
@@ -107,7 +107,9 @@
     tile_x, tile_y, depth = (speed.shape[1], speed.shape[2], speed.shape[3])
     stripes = aperture.shape[1]
     mine = aperture[0]
-    lists = lax.all_gather(aperture, "tile", axis=0, tiled=True)
+    lists = jnp.concatenate(
+        lax.all_to_all(jnp.stack([aperture] * lax.axis_size("tile")), "tile", 0, 0), axis=0
+    )
     owner_ids = jnp.arange(owners, dtype=jnp.int32)
     held_ids = jnp.arange(held, dtype=jnp.int32)
     matches = (lists // held == myself)[:, :, None] & (

time: 307 us -> 291 us (0.948)
  blocking collectives: 29 us -> 0 us
  starting transfers between devices: 12.4 us -> 20.1 us
  waiting for transfers between devices: 181 us -> 185 us
    all_gather x1 -> x0, blocking collectives: 29 us -> none  [per_device(): lists = lax.all_gather(aperture, 'tile', axis=0, tiled=True)]
    all_to_all x1, waiting for transfers between devices: 0.01 us -> 12.4 us  [per_device(): lax.all_to_all(back_buoy, 'tile', split_axis=0, concat_axis=0, tiled=True)]
    all_gather x1, waiting for transfers between devices: 48.1 us -> 39.3 us  [per_device(): lax.all_gather(density, 'tile', axis=0, tiled=True)]
    all_to_all x0 -> x1, starting transfers between devices: none -> 7.62 us  [per_device(): lax.all_to_all(jnp.stack([aperture] * lax.axis_size('tile')), 'tile', 0, 0)]
  transfers between devices with their start and end apart: 5 -> 6, of which waited for: 4 -> 5; matrix products, arithmetic and copies ran while one was open for 6% -> 23% of each run, Pallas kernels for 0% -> 0%
where the time goes in v1:
time: 291 us; the launch traced here: 290 us
  waiting for transfers between devices  185 us (64%)
  other arithmetic  45.3 us (16%)
  starting transfers between devices  20.1 us (7%)
  matrix products  17.3 us (6%)
  between operations  14.1 us (5%)
  local copies, waits for them, and re-layouts  8.48 us (3%)
    psum x1, waiting for transfers between devices, per_device(): bulk_sum, buoy_sum = lax.psum((own_bulk, own_buoy), 'grp')  73.1 us
    all_gather x1, waiting for transfers between devices, per_device(): lax.all_gather(speed, 'tile', axis=0, tiled=True)  47.1 us
    all_gather x1, waiting for transfers between devices, per_device(): lax.all_gather(density, 'tile', axis=0, tiled=True)  39.3 us
    add x1, other arithmetic, evolve(): bulk_image = bulk_image + changes[step_index][0] * adj_pressure  14.1 us
    all_to_all x1, waiting for transfers between devices, per_device(): lax.all_to_all(back_buoy, 'tile', split_axis=0, concat_axis=0, tiled=True)  12.4 us
    all_to_all x1, waiting for transfers between devices, per_device(): lax.all_to_all(back_bulk, 'tile', split_axis=0, concat_axis=0, tiled=True)  11.9 us
    add x6, other arithmetic, advance(): return (pressure + bulk * divergence + source, moved)  11.2 us
    add x3, other arithmetic, advance(): velocity[which_dim] + buoyancy * forward_diff(pressure, which_dim)  8.67 us
  transfers between devices with their start and end apart: 6, of which 5 were waited for; matrix products, arithmetic and copies ran while one was open for 23% of the time, Pallas kernels for 0%

profile of v1, /device:TPU:2, one launch (start us, length us, event | category | flops | bytes accessed | tf_op | source)
XLA Modules:
  0.0 290.3 jit_solution(6312812882319876394)
XLA Ops:
  7.2 0.0 copy-start.7
  7.2 0.0 copy-start.8
  7.2 0.0 copy-start.6
  7.2 0.0 copy-start.10
  7.2 0.0 copy-start.9
  7.2 0.0 all-gather.3.cloned.1.call-start
  7.3 0.7 all-gather.3.cloned.1.call-update
  7.9 0.0 all-gather.5.cloned.1.call-start
  8.0 0.7 all-gather.5.cloned.1.call-update
  8.7 1.3 stack.2
  10.0 7.6 %all-to-all-start = ((s32[32,1,16]{2,1,0:T(1,128)}), s32[32,1,16]{2,1,0:T(1,128)S(1)}, u32[]{:S(2)}, u32[]{:S(2)}) async-start(s32[32,1,16]{2,1,0:T(1,128)} %stack.2), calls=%async_computation | async-start | bytes 32768 | tf_op jit(solution)/shard_map/all_to_all | solution.py:111
  17.6 1.5 convert_element_type.67
  19.1 1.5 convert_element_type.68
  20.6 0.0 copy-done.8
  20.6 0.0 copy-start
  20.6 0.7 fusion.658
  21.4 0.6 iota_compare_fusion.5
  22.0 1.3 iota_compare_fusion.6
  23.3 0.6 fusion.657
  24.0 0.0 copy-done.9
  24.0 0.1 iota_compare_fusion.1
  24.0 0.1 iota_compare_fusion.2
  24.1 0.1 broadcast_and_fusion
  24.2 0.9 slice_bitcast_fusion.3
  25.1 39.3 %all-gather.3.cloned.1.call-done = f32[128,2,32,128]{3,2,1,0:T(8,128)} async-done(((f32[4,2,32,128]{3,2,1,0:T(8,128)}), f32[128,2,32,128]{3,2,1,0:T(8,128)}) %all-gather.3.cloned.1.call-update) | async-done | bytes 4194320 | tf_op jit(solution)/shard_map/all_gather | solution.py:123
  64.4 5.8 %fusion.2 = f32[16,2,32,128]{3,0,2,1:T(8,128)S(1)} fusion(f32[128,2,32,128]{3,2,1,0:T(8,128)} %all-gather.3.cloned.1.call-done, s32[16]{0:T(128)S(1)} %bitcast.173), kind=kOutput, calls=%fused_computation.2 | convolution fusion | flops 201328640 | bytes 4718656 | tf_op jit(solution)/shard_map/jt,txyz->jxyz/dot_general | solution.py:128
  70.2 0.2 copy.91
  70.4 47.1 %all-gather.5.cloned.1.call-done = f32[128,2,32,128]{3,2,1,0:T(8,128)} async-done(((f32[4,2,32,128]{3,2,1,0:T(8,128)}), f32[128,2,32,128]{3,2,1,0:T(8,128)}) %all-gather.5.cloned.1.call-update) | async-done | bytes 4194320 | tf_op jit(solution)/shard_map/all_gather | solution.py:122
  117.5 6.0 %fusion = f32[16,2,32,128]{3,0,2,1:T(8,128)S(1)} fusion(f32[128,2,32,128]{3,2,1,0:T(8,128)} %all-gather.5.cloned.1.call-done, s32[16]{0:T(128)S(1)} %bitcast.174), kind=kOutput, calls=%fused_computation | convolution fusion | flops 201328640 | bytes 4718656 | tf_op jit(solution)/shard_map/jt,txyz->jxyz/dot_general | solution.py:127
  123.5 0.2 copy.93
  123.7 2.8 fusion.540
  126.5 2.3 fusion.30
  128.8 1.6 fusion.247
  130.4 3.0 %fusion.313 = (f32[32,32,128]{2,1,0:T(8,128)S(1)}, f32[32,32,128]{2,1,0:T(8,128)S(1)}, f32[32,32,128]{2,1,0:T(8,128)S(1)}, f32[32,32,128]{2,1,0:T(8,128)S(1)}, f...) fusion(f32[32,32,128]{2,1,0:T(8,128)S(1)} %get-tuple-element.27, f32[32,32,128]{2,1,0:T(8,128)S(1)} %fusion.247, ...), kind=kLoop, calls=%fused_computation.658 | loop fusion | flops 10354688 | bytes 7864320 | tf_op jit(solution)/shard_map/add | solution.py:41
  133.4 1.6 fusion.300
  135.0 2.2 fusion.83
  137.1 2.8 fusion.337
  140.0 1.6 fusion.353
  141.6 2.1 fusion.136
  143.6 4.9 %multiply_add_fusion = (f32[32,32,128]{2,1,0:T(8,128)}, f32[32,32,128]{2,1,0:T(8,128)}, f32[32,32,128]{2,1,0:T(8,128)}, f32[32,32,128]{2,1,0:T(8,128)}, f32[32,3...) fusion(f32[32,32,128]{2,1,0:T(8,128)S(1)} %get-tuple-element.51, ...), kind=kLoop, calls=%fused_computation.988 | loop fusion | flops 14942208 | bytes 16252928 | tf_op jit(solution)/shard_map/add | solution.py:95
  148.6 14.1 %fusion.194 = f32[32,32,128]{2,1,0:T(8,128)S(1)} fusion(f32[32,32,128]{2,1,0:T(8,128)S(1)} %fusion.247, f32[32,32,128]{2,1,0:T(8,128)S(1)} %fusion.136, f32[32,32,128]{2,1,0:T(8,128)S(1)} %get-tuple-element.24, f32[32,32,128]{2,1,0:T(8,128)} %get-tuple-element.22, f32[32,32,128]{2,1,0:T(8,128)} %get-tuple-element.21, f32[32,32,128]{2,1,0:T(8,128)S(1)} %fusion.353, ...), kind=kLoop, calls=%fused_computation.539 | loop fusion | flops 11927552 | bytes 7870724 | tf_op jit(solution)/shard_map/add | solution.py:92
  162.7 0.0 copy-start.2
  162.7 0.9 fusion.632
  163.6 1.6 copy.95
  165.2 0.0 all-to-all-done
  165.2 5.9 %all-to-all-start.1 = ((f32[32,2,32,128]{3,2,1,0:T(8,128)}), f32[32,2,32,128]{3,2,1,0:T(8,128)S(1)}, u32[]{:S(2)}, u32[]{:S(2)}) async-start(f32[32,2,32,128]{3,2,1,0:T(8,128)} %copy.95), calls=%async_computation.1 | async-start | bytes 2097152 | tf_op jit(solution)/shard_map/all_to_all | solution.py:146
  171.1 0.0 copy-done.2
  171.1 0.0 copy-start.4
  171.1 0.0 copy-start.5
  171.1 0.9 fusion.630
  172.0 1.6 copy.102
  173.6 11.9 %all-to-all-done.1 = f32[32,2,32,128]{3,2,1,0:T(8,128)S(1)} async-done(((f32[32,2,32,128]{3,2,1,0:T(8,128)}), f32[32,2,32,128]{3,2,1,0:T(8,128)S(1)}, u32[]{:S(2)}, u32[]{:S(2)}) %all-to-all-start.1) | async-done | bytes 1048608 | tf_op jit(solution)/shard_map/all_to_all | solution.py:146
  185.5 6.4 %all-to-all-start.2 = ((f32[32,2,32,128]{3,2,1,0:T(8,128)}), f32[32,2,32,128]{3,2,1,0:T(8,128)S(1)}, u32[]{:S(2)}, u32[]{:S(2)}) async-start(f32[32,2,32,128]{3,2,1,0:T(8,128)} %copy.102), calls=%async_computation.2 | async-start | bytes 2097152 | tf_op jit(solution)/shard_map/all_to_all | solution.py:147
  191.9 0.0 all-reduce.51.cloned.1.call-start
  192.0 0.1 copy.89
  192.1 1.8 fusion.6
  194.0 12.4 %all-to-all-done.2 = f32[32,2,32,128]{3,2,1,0:T(8,128)S(1)} async-done(((f32[32,2,32,128]{3,2,1,0:T(8,128)}), f32[32,2,32,128]{3,2,1,0:T(8,128)S(1)}, u32[]{:S(2)}, u32[]{:S(2)}) %all-to-all-start.2) | async-done | bytes 1048608 | tf_op jit(solution)/shard_map/all_to_all | solution.py:147
  206.4 1.8 fusion.4
  208.2 0.0 all-reduce.51.cloned.1.call-update
  208.2 73.1 %all-reduce.51.cloned.1.call-done = (f32[4,2,32,128]{3,0,2,1:T(4,128)}, f32[4,2,32,128]{3,0,2,1:T(4,128)}) async-done(((f32[4,2,32,128]{3,0,2,1:T(4,128)}, f32[4,2,32,128]{3,0,2,1:T(4,128)}), (f32[4,2,32,128]{3,0,2,1:T(4,128)}, f32[4,2,32,128]{3,0,2,1:T(4,128)})) %all-reduce.51.cloned.1.call-update) | async-done | bytes 262160 | tf_op jit(solution)/shard_map/psum | solution.py:151
  281.3 0.0 copy-done.4
  281.3 1.2 subtract_multiply_fusion
  282.5 0.7 copy.106
  283.2 0.7 copy.107
  (15 shorter events, 0.1 us)
Async XLA Ops:
  7.2 16.8 %copy-start.7 = (s32[1,16]{1,0:T(1,128)S(1)}, s32[1,16]{1,0:T(1,128)}, u32[]{:S(2)}) copy-start(s32[1,16]{1,0:T(1,128)} %param.13) | copy-start | bytes 196
  7.2 13.5 %copy-start.8 = (s32[1,3]{1,0:T(1,128)S(1)}, s32[1,3]{1,0:T(1,128)}, u32[]{:S(2)}) copy-start(s32[1,3]{1,0:T(1,128)} %param.14) | copy-start | bytes 40
  7.2 16.1 %copy-start.6 = (f32[1,4]{1,0:T(1,128)S(1)}, f32[1,4]{1,0:T(1,128)}, u32[]{:S(2)}) copy-start(f32[1,4]{1,0:T(1,128)} %param.15) | copy-start | bytes 52
  7.2 16.7 %copy-start.10 = (s32[1,32,2]{1,2,0:T(2,128)S(1)}, s32[1,32,2]{1,2,0:T(2,128)}, u32[]{:S(2)}) copy-start(s32[1,32,2]{1,2,0:T(2,128)} %param.16) | copy-start | bytes 772
  7.2 16.7 %copy-start.9 = (f32[1,4,32]{2,1,0:T(4,128)S(1)}, f32[1,4,32]{2,1,0:T(4,128)}, u32[]{:S(2)}) copy-start(f32[1,4,32]{2,1,0:T(4,128)} %param.17) | copy-start | bytes 1540
  7.2 57.1 %all-gather.3.cloned.1.call-start = ((), (), s32[]{:S(2)}) async-start(), calls=%async_computation.3 | async-start | bytes 4325376 | tf_op jit(solution)/shard_map/all_gather | solution.py:123
  7.9 109.5 %all-gather.5.cloned.1.call-start = ((), (), s32[]{:S(2)}) async-start(), calls=%async_computation.4 | async-start | bytes 4325376 | tf_op jit(solution)/shard_map/all_gather | solution.py:122
  10.0 155.2 %all-to-all-start = ((s32[32,1,16]{2,1,0:T(1,128)}), s32[32,1,16]{2,1,0:T(1,128)S(1)}, u32[]{:S(2)}, u32[]{:S(2)}) async-start(s32[32,1,16]{2,1,0:T(1,128)} %stack.2), calls=%async_computation | async-start | bytes 32768 | tf_op jit(solution)/shard_map/all_to_all | solution.py:111
  20.6 3.6 %copy-start = (f32[1,4,32,32,128]{4,3,2,1,0:T(8,128)}, f32[1,4,32,32,128]{4,3,2,1,0:T(8,128)S(1)}, u32[]{:S(2)}) copy-start(f32[1,4,32,32,128]{4,3,2,1,0:T(8,128)S(1)} %convert_element_type.68) | copy-start | bytes 6291460
  117.5 6.2 %copy-start.1 = (f32[1,4,32,32,128]{4,3,2,1,0:T(8,128)S(1)}, f32[1,4,32,32,128]{4,3,2,1,0:T(8,128)}, u32[]{:S(2)}) copy-start(f32[1,4,32,32,128]{4,3,2,1,0:T(8,128)} %copy-done) | copy-start | bytes 6291460
  117.5 6.2 %copy-start.3 = (f32[32,32,128]{2,1,0:T(8,128)S(1)}, f32[32,32,128]{2,1,0:T(8,128)}, u32[]{:S(2)}) copy-start(f32[32,32,128]{2,1,0:T(8,128)} %get-tuple-element.68) | copy-start | bytes 1572868
  162.7 8.4 %copy-start.2 = (f32[32,32,128]{2,1,0:T(8,128)S(1)}, f32[32,32,128]{2,1,0:T(8,128)}, u32[]{:S(2)}) copy-start(f32[32,32,128]{2,1,0:T(8,128)} %get-tuple-element.16) | copy-start | bytes 1572868
  165.2 20.3 %all-to-all-start.1 = ((f32[32,2,32,128]{3,2,1,0:T(8,128)}), f32[32,2,32,128]{3,2,1,0:T(8,128)S(1)}, u32[]{:S(2)}, u32[]{:S(2)}) async-start(f32[32,2,32,128]{3,2,1,0:T(8,128)} %copy.95), calls=%async_computation.1 | async-start | bytes 2097152 | tf_op jit(solution)/shard_map/all_to_all | solution.py:146
  171.1 110.2 %copy-start.4 = (f32[4,2,32,128]{3,2,1,0:T(8,128)S(1)}, f32[4,2,32,128]{3,2,1,0:T(8,128)}, u32[]{:S(2)}) copy-start(f32[4,2,32,128]{3,2,1,0:T(8,128)} %param.10) | copy-start | bytes 393220
  171.1 110.2 %copy-start.5 = (f32[4,2,32,128]{3,2,1,0:T(8,128)S(1)}, f32[4,2,32,128]{3,2,1,0:T(8,128)}, u32[]{:S(2)}) copy-start(f32[4,2,32,128]{3,2,1,0:T(8,128)} %param.9) | copy-start | bytes 393220
  185.5 20.9 %all-to-all-start.2 = ((f32[32,2,32,128]{3,2,1,0:T(8,128)}), f32[32,2,32,128]{3,2,1,0:T(8,128)S(1)}, u32[]{:S(2)}, u32[]{:S(2)}) async-start(f32[32,2,32,128]{3,2,1,0:T(8,128)} %copy.102), calls=%async_computation.2 | async-start | bytes 2097152 | tf_op jit(solution)/shard_map/all_to_all | solution.py:147
  191.9 89.3 %all-reduce.51.cloned.1.call-start = ((), (), s32[]{:S(2)}) async-start(), calls=%async_computation.5 | async-start | bytes 524288 | tf_op jit(solution)/shard_map/psum | solution.py:151
Sparse Core Ops, SparseCore 0:
  10.6 53.7 all-gather.2
  66.9 50.5 all-gather.4
  208.4 72.8 all-reduce.50
